TPU v7x, 32 devices: a whole 2x2x4 slice. The times are simulated.
32 devices in a mesh: shot: 2 (over x), gx: 16 (over z, y, core).
Axes of the slice: x: 2, y: 2, z: 4, core: 2. Of those that a mesh axis runs over, the one named last changes fastest.
Arguments:
- adjoint_now: float32 [32, 16, 32, 128], P(('shot', 'gx')), parts along dimension 0, may hold values from -6 to 6
- adjoint_before: float32 [32, 16, 32, 128], P(('shot', 'gx')), parts along dimension 0, may hold values from -6 to 6
- vel_coeff: float32 [16, 16, 32, 128], P('gx'), may hold values from 0.04 to 0.18
- forward_accel: bfloat16 [8, 16, 16, 32, 128], P('shot', 'gx'), parts along dimension 0, may hold values from -6 to 6
- residual: float32 [8, 32768], P('shot', 'gx'), parts along dimension 0, may hold values from -6 to 6
- rec_cell: int32 [32768], P('gx'), may hold values from 0 to 65535
- owner_list: int32 [256, 384], P('gx'), may hold values from -1 to 2047, as said below
- trace_count: int32 [32], P(('shot', 'gx')), parts along dimension 0, may hold values from 1024 to 2048, as said below
Outputs:
- adjoint_final: float32 [32, 16, 32, 128], P(('shot', 'gx')), parts along dimension 0
- adjoint_prior: float32 [32, 16, 32, 128], P(('shot', 'gx')), parts along dimension 0
- gradient: float32 [32, 16, 32, 128], P(('shot', 'gx')), parts along dimension 0
There are 2 independent parts, one for each index of `shot`. A program takes and returns all parts, laid end to end along the dimension named above; an argument that names none is the same for every part. Nothing has to cross between parts.
Inputs may be any that keep to these rules, and one draw needn't show every extreme that they name: `owner_list`: row d * 16 + e holds in some of its 384 slots the local indices of device d's traces owned by pencil e, and -1 in the other slots; each local index 0 to 2047 of a device stands exactly once in that device's 16 rows. Traces 0 to trace_count[d] - 1 of device d are live; the others carry no source.
All inputs are finite; a program needn't handle non-finite values.
Results may differ from a plain program's by a relative error of at most 0.0003.
Values sent between devices are 32-bit elements; how exact they have to be, the bound alone decides.
A program may use at most 256 MiB of HBM per device.

v0:
```python
import jax
import jax.numpy as jnp
from jax import lax
from jax.sharding import PartitionSpec as P

PY = 4


weights = (-205.0 / 72.0, 8.0 / 5.0, -1.0 / 5.0, 8.0 / 315.0, -1.0 / 560.0)


def passed_along(array, axis, by):
    size = lax.axis_size(axis)
    pairs = [(i, i + by) for i in range(size) if 0 <= i + by < size]
    return lax.ppermute(array, axis, pairs)


def neighbours(present):
    position = lax.axis_index("gx") % PY
    lower_mask = (position > 0).astype(jnp.float32)
    upper_mask = (position < PY - 1).astype(jnp.float32)
    lower_x = passed_along(present[-4:], "gx", PY)
    upper_x = passed_along(present[:4], "gx", -PY)
    lower_y = passed_along(present[:, -4:], "gx", 1) * lower_mask
    upper_y = passed_along(present[:, :4], "gx", -1) * upper_mask
    return (lower_x, upper_x, lower_y, upper_y)


def per_device(
    adjoint_now,
    adjoint_before,
    vel_coeff,
    forward_accel,
    residual,
    rec_cell,
    owner_list,
    trace_count,
):
    step_count = forward_accel.shape[0]
    extent_first, extent_second, extent_third = (
        forward_accel.shape[2],
        forward_accel.shape[3],
        forward_accel.shape[4],
    )
    traces = residual.shape[1]
    owners = owner_list.shape[0]
    cell_count = extent_first * extent_second * extent_third
    living = jnp.arange(traces, dtype=jnp.int32) < trace_count[0]
    residual_kept = jnp.where(living[None, :], residual, 0.0)
    filled = owner_list >= 0
    owner_ids = jnp.broadcast_to(jnp.arange(owners, dtype=jnp.int32)[:, None], owner_list.shape)
    where_listed = jnp.where(filled, owner_list, traces).reshape(-1)
    owner_of = (
        jnp.zeros((traces,), jnp.int32).at[where_listed].set(owner_ids.reshape(-1), mode="drop")
    )
    places = jnp.stack([rec_cell, owner_of]).astype(jnp.float32)
    gathered, gathered_place = (
        lax.all_gather(residual_kept, "gx", axis=1, tiled=True),
        lax.all_gather(places, "gx", axis=1, tiled=True),
    )
    owned = gathered_place[1].astype(jnp.int32) == lax.axis_index("gx")
    values = jnp.where(owned[None, :], gathered, 0.0)
    target = gathered_place[0].astype(jnp.int32)
    sources = jnp.zeros((step_count, cell_count), jnp.float32).at[:, target].add(values)
    sources = sources.reshape(step_count, extent_first, extent_second, extent_third)
    present = adjoint_now[0]
    before = adjoint_before[0]
    velocity = vel_coeff[0]
    gradient = jnp.zeros_like(present)
    for moment in range(step_count):
        lower_x, upper_x, lower_y, upper_y = neighbours(present)
        wide_first = jnp.concatenate([lower_x, present, upper_x], axis=0)
        wide_second = jnp.concatenate([lower_y, present, upper_y], axis=1)
        padded = jnp.pad(present, ((0, 0), (0, 0), (4, 4)))
        curvature = 3.0 * weights[0] * present
        for offset in range(1, 5):
            pairs = (
                wide_first[4 + offset : 4 + offset + extent_first]
                + wide_first[4 - offset : 4 - offset + extent_first]
            )
            pairs = (
                pairs
                + wide_second[:, 4 + offset : 4 + offset + extent_second]
                + wide_second[:, 4 - offset : 4 - offset + extent_second]
            )
            pairs = (
                pairs
                + padded[:, :, 4 + offset : 4 + offset + extent_third]
                + padded[:, :, 4 - offset : 4 - offset + extent_third]
            )
            curvature = curvature + weights[offset] * pairs
        following = 2.0 * present - before + velocity * curvature + sources[moment]
        gradient = gradient + following * forward_accel[moment, 0].astype(jnp.float32)
        before = present
        present = following
    return (present[None], before[None], gradient[None])


def solution(mesh):
    in_specs = (
        P(("shot", "gx"), None, None, None),
        P(("shot", "gx"), None, None, None),
        P("gx", None, None, None),
        P("shot", "gx", None, None, None),
        P("shot", "gx"),
        P("gx"),
        P("gx", None),
        P(("shot", "gx")),
    )
    out_specs = (
        P(("shot", "gx"), None, None, None),
        P(("shot", "gx"), None, None, None),
        P(("shot", "gx"), None, None, None),
    )
    return jax.shard_map(
        per_device, mesh=mesh, in_specs=in_specs, out_specs=out_specs, check_vma=False
    )
```

profile of v0, /device:TPU:1, one launch (start us, length us, event | category | flops | bytes accessed | tf_op | source)
XLA Modules:
  0.0 392.3 jit_solution(1994902201644918610)
XLA Ops:
  0.6 0.9 slice_bitcast_fusion.1
  1.5 4.0 %collective-permute-start.1 = (f32[4,32,128]{2,1,0:T(8,128)S(1)}, f32[4,32,128]{2,1,0:T(8,128)S(1)}, u32[]{:S(2)}, u32[]{:S(2)}) collective-permute-start(f32[4,32,128]{2,1,0:T(8,128)S(1)} %get-tuple-element.24), channel_id=1, source_target_pairs={{0,4},{1,5},{2,6},{3,7},{4,8},{5,9},{6,10},{7,11},{8,12},{9,13},{1... | collective-permute-start | bytes 196616 | tf_op jit(solution)/shard_map/ppermute | solution.py:15
  5.6 1.3 collective-permute-start
  6.9 0.9 fusion.189
  7.7 4.0 %collective-permute-start.3 = (f32[16,4,128]{2,1,0:T(4,128)S(1)}, f32[16,4,128]{2,1,0:T(4,128)S(1)}, u32[]{:S(2)}, u32[]{:S(2)}) collective-permute-start(f32[16,4,128]{2,1,0:T(4,128)S(1)} %get-tuple-element.22), channel_id=1, source_target_pairs={{0,1},{1,2},{2,3},{3,4},{4,5},{5,6},{6,7},{7,8},{8,9},{9,10},{10,1... | collective-permute-start | bytes 98312 | tf_op jit(solution)/shard_map/ppermute | solution.py:15
  11.7 1.9 collective-permute-start.2
  13.7 0.7 fusion.179
  14.5 23.0 %scatter_custom_fusion = s32[2048]{0:T(1024)S(1)} fusion(s32[6144]{0:T(1024)S(1)} %bitcast.96, s32[6144]{0:T(1024)S(1)} %reshape.93, s32[]{:T(128)} %constant.18.clone.1), kind=kCustom, calls=%fused_computation.355 | custom fusion | bytes 8196 | tf_op jit(solution)/shard_map/scatter | solution.py:54
  37.5 0.7 add_convert_fusion
  38.2 23.9 %all_gather.6 = f32[2,32768]{1,0:T(2,128)S(1)} all-gather(f32[2,2048]{1,0:T(2,128)S(1)} %add_convert_fusion), channel_id=1, replica_groups=mesh['shot'=2,'gx'=16] {'gx'}, dimensions={1}, use_global_device_ids=true | all-gather | bytes 278528 | tf_op jit(solution)/shard_map/all_gather | solution.py:59
  62.9 0.8 broadcast_select_fusion
  63.7 18.9 %all_gather.7 = f32[4,32768]{1,0:T(4,128)S(1)} all-gather(f32[4,2048]{1,0:T(4,128)S(1)} %broadcast_select_fusion), channel_id=1, replica_groups=mesh['shot'=2,'gx'=16] {'gx'}, dimensions={1}, use_global_device_ids=true | all-gather | bytes 557056 | tf_op jit(solution)/shard_map/all_gather | solution.py:58
  83.3 8.4 %copy.12 = f32[32768,4]{1,0:T(8,128)} copy(f32[32768,4]{0,1:T(4,128)S(1)} %select_bitcast_fusion) | data formatting | bytes 1048576 | tf_op jit(solution)/shard_map/jit(_where)/select_n | solution.py:62
  91.7 187.4 %scatter_custom_fusion.1 = f32[4,65536]{0,1:T(8,128)} fusion(s32[32768]{0:T(1024)S(1)} %bitcast.85, f32[32768,4]{1,0:T(8,128)} %copy.12, f32[]{:T(128)} %constant.21.clone.1), kind=kCustom, calls=%fused_computation.6 | custom fusion | flops 131072 | bytes 1049088 | tf_op jit(solution)/shard_map/scatter-add | solution.py:64
  279.1 72.3 %slice_reduce_fusion.3 = (f32[65536]{0:T(1024)S(1)}, f32[65536]{0:T(1024)S(1)}, f32[65536]{0:T(1024)S(1)}, f32[65536]{0:T(1024)S(1)}) fusion(f32[4,65536]{0,1:T(8,128)} %scatter_custom_fusion.1), kind=kLoop, calls=%fused_computation.5 | loop fusion | bytes 2097152 | tf_op jit(solution)/shard_map/slice | solution.py:92
  352.3 3.4 collective-permute-start.7
  355.7 1.3 collective-permute-start.5
  357.0 1.3 collective-permute-start.4
  358.3 1.9 collective-permute-start.6
  360.2 3.3 collective-permute-done.6
  363.5 0.6 fusion.85
  364.2 1.9 collective-permute-start.11
  366.2 4.0 %collective-permute-start.9 = (f32[4,32,128]{2,1,0:T(8,128)S(1)}, f32[4,32,128]{2,1,0:T(8,128)S(1)}, u32[]{:S(2)}, u32[]{:S(2)}) collective-permute-start(f32[4,32,128]{2,1,0:T(8,128)S(1)} %get-tuple-element.16), channel_id=1, source_target_pairs={{0,4},{1,5},{2,6},{3,7},{4,8},{5,9},{6,10},{7,11},{8,12},{9,13},{1... | collective-permute-start | bytes 196616 | tf_op jit(solution)/shard_map/ppermute | solution.py:15
  370.2 1.3 collective-permute-start.8
  371.5 2.7 collective-permute-start.10
  374.2 2.5 collective-permute-done.10
  377.4 3.0 collective-permute-start.15
  380.5 1.9 collective-permute-start.14
  382.4 3.4 collective-permute-start.13
  385.8 1.3 collective-permute-start.12
  387.2 3.7 collective-permute-done.12
  390.8 1.5 fusion.175
  (47 shorter events, 2.4 us)
Async XLA Ops:
  1.5 350.0 %collective-permute-start.1 = (f32[4,32,128]{2,1,0:T(8,128)S(1)}, f32[4,32,128]{2,1,0:T(8,128)S(1)}, u32[]{:S(2)}, u32[]{:S(2)}) collective-permute-start(f32[4,32,128]{2,1,0:T(8,128)S(1)} %get-tuple-element.24), channel_id=1, source_target_pairs={{0,4},{1,5},{2,6},{3,7},{4,8},{5,9},{6,10},{7,11},{8,12},{9,13},{1... | collective-permute-start | bytes 196616 | tf_op jit(solution)/shard_map/ppermute | solution.py:15
  5.6 346.0 %collective-permute-start = (f32[4,32,128]{2,1,0:T(8,128)S(1)}, f32[4,32,128]{2,1,0:T(8,128)S(1)}, u32[]{:S(2)}, u32[]{:S(2)}) collective-permute-start(f32[4,32,128]{2,1,0:T(8,128)S(1)} %get-tuple-element.23), channel_id=1, source_target_pairs={{4,0},{5,1},{6,2},{7,3},{8,4},{9,5},{10,6},{11,7},{12,8},{13,9},{1... | collective-permute-start | bytes 196616 | tf_op jit(solution)/shard_map/ppermute | solution.py:15
  7.7 343.8 %collective-permute-start.3 = (f32[16,4,128]{2,1,0:T(4,128)S(1)}, f32[16,4,128]{2,1,0:T(4,128)S(1)}, u32[]{:S(2)}, u32[]{:S(2)}) collective-permute-start(f32[16,4,128]{2,1,0:T(4,128)S(1)} %get-tuple-element.22), channel_id=1, source_target_pairs={{0,1},{1,2},{2,3},{3,4},{4,5},{5,6},{6,7},{7,8},{8,9},{9,10},{10,1... | collective-permute-start | bytes 98312 | tf_op jit(solution)/shard_map/ppermute | solution.py:15
  11.7 339.8 %collective-permute-start.2 = (f32[16,4,128]{2,1,0:T(4,128)S(1)}, f32[16,4,128]{2,1,0:T(4,128)S(1)}, u32[]{:S(2)}, u32[]{:S(2)}) collective-permute-start(f32[16,4,128]{2,1,0:T(4,128)S(1)} %get-tuple-element.21), channel_id=1, source_target_pairs={{1,0},{2,1},{3,2},{4,3},{5,4},{6,5},{7,6},{8,7},{9,8},{10,9},{11,1... | collective-permute-start | bytes 98312 | tf_op jit(solution)/shard_map/ppermute | solution.py:15
  279.1 72.4 %copy-start = (f32[1,16,32,128]{3,2,1,0:T(8,128)S(1)}, f32[1,16,32,128]{3,2,1,0:T(8,128)}, u32[]{:S(2)}) copy-start(f32[1,16,32,128]{3,2,1,0:T(8,128)} %param.10) | copy-start | bytes 786436
  279.1 72.5 %copy-start.2 = (f32[1,16,32,128]{3,2,1,0:T(8,128)S(1)}, f32[1,16,32,128]{3,2,1,0:T(8,128)}, u32[]{:S(2)}) copy-start(f32[1,16,32,128]{3,2,1,0:T(8,128)} %param.8) | copy-start | bytes 786436
  279.1 72.5 %copy-start.4 = (f32[1,16,32,128]{3,2,1,0:T(8,128)S(1)}, f32[1,16,32,128]{3,2,1,0:T(8,128)}, u32[]{:S(2)}) copy-start(f32[1,16,32,128]{3,2,1,0:T(8,128)} %param.9) | copy-start | bytes 786436
  279.1 111.7 %copy-start.3 = (bf16[4,1,16,32,128]{4,3,2,1,0:T(8,128)(2,1)S(1)}, bf16[4,1,16,32,128]{4,3,2,1,0:T(8,128)(2,1)}, u32[]{:S(2)}) copy-start(bf16[4,1,16,32,128]{4,3,2,1,0:T(8,128)(2,1)} %param.11) | copy-start | bytes 1572868
  352.3 8.0 %collective-permute-start.7 = (f32[16,4,128]{2,1,0:T(4,128)S(1)}, f32[16,4,128]{2,1,0:T(4,128)S(1)}, u32[]{:S(2)}, u32[]{:S(2)}) collective-permute-start(f32[16,4,128]{2,1,0:T(4,128)S(1)} %get-tuple-element.18), channel_id=1, source_target_pairs={{0,1},{1,2},{2,3},{3,4},{4,5},{5,6},{6,7},{7,8},{8,9},{9,10},{10,1... | collective-permute-start | bytes 98312 | tf_op jit(solution)/shard_map/ppermute | solution.py:15
  355.7 7.8 %collective-permute-start.5 = (f32[4,32,128]{2,1,0:T(8,128)S(1)}, f32[4,32,128]{2,1,0:T(8,128)S(1)}, u32[]{:S(2)}, u32[]{:S(2)}) collective-permute-start(f32[4,32,128]{2,1,0:T(8,128)S(1)} %get-tuple-element.20), channel_id=1, source_target_pairs={{0,4},{1,5},{2,6},{3,7},{4,8},{5,9},{6,10},{7,11},{8,12},{9,13},{1... | collective-permute-start | bytes 196616 | tf_op jit(solution)/shard_map/ppermute | solution.py:15
  357.0 6.5 %collective-permute-start.4 = (f32[4,32,128]{2,1,0:T(8,128)S(1)}, f32[4,32,128]{2,1,0:T(8,128)S(1)}, u32[]{:S(2)}, u32[]{:S(2)}) collective-permute-start(f32[4,32,128]{2,1,0:T(8,128)S(1)} %get-tuple-element.19), channel_id=1, source_target_pairs={{4,0},{5,1},{6,2},{7,3},{8,4},{9,5},{10,6},{11,7},{12,8},{13,9},{1... | collective-permute-start | bytes 196616 | tf_op jit(solution)/shard_map/ppermute | solution.py:15
  358.3 5.2 %collective-permute-start.6 = (f32[16,4,128]{2,1,0:T(4,128)S(1)}, f32[16,4,128]{2,1,0:T(4,128)S(1)}, u32[]{:S(2)}, u32[]{:S(2)}) collective-permute-start(f32[16,4,128]{2,1,0:T(4,128)S(1)} %get-tuple-element.17), channel_id=1, source_target_pairs={{1,0},{2,1},{3,2},{4,3},{5,4},{6,5},{7,6},{8,7},{9,8},{10,9},{11,1... | collective-permute-start | bytes 98312 | tf_op jit(solution)/shard_map/ppermute | solution.py:15
  364.2 9.9 %collective-permute-start.11 = (f32[16,4,128]{2,1,0:T(4,128)S(1)}, f32[16,4,128]{2,1,0:T(4,128)S(1)}, u32[]{:S(2)}, u32[]{:S(2)}) collective-permute-start(f32[16,4,128]{2,1,0:T(4,128)S(1)} %get-tuple-element.14), channel_id=1, source_target_pairs={{0,1},{1,2},{2,3},{3,4},{4,5},{5,6},{6,7},{7,8},{8,9},{9,10},{10,1... | collective-permute-start | bytes 98312 | tf_op jit(solution)/shard_map/ppermute | solution.py:15
  366.2 10.5 %collective-permute-start.9 = (f32[4,32,128]{2,1,0:T(8,128)S(1)}, f32[4,32,128]{2,1,0:T(8,128)S(1)}, u32[]{:S(2)}, u32[]{:S(2)}) collective-permute-start(f32[4,32,128]{2,1,0:T(8,128)S(1)} %get-tuple-element.16), channel_id=1, source_target_pairs={{0,4},{1,5},{2,6},{3,7},{4,8},{5,9},{6,10},{7,11},{8,12},{9,13},{1... | collective-permute-start | bytes 196616 | tf_op jit(solution)/shard_map/ppermute | solution.py:15
  370.2 6.6 %collective-permute-start.8 = (f32[4,32,128]{2,1,0:T(8,128)S(1)}, f32[4,32,128]{2,1,0:T(8,128)S(1)}, u32[]{:S(2)}, u32[]{:S(2)}) collective-permute-start(f32[4,32,128]{2,1,0:T(8,128)S(1)} %get-tuple-element.15), channel_id=1, source_target_pairs={{4,0},{5,1},{6,2},{7,3},{8,4},{9,5},{10,6},{11,7},{12,8},{13,9},{1... | collective-permute-start | bytes 196616 | tf_op jit(solution)/shard_map/ppermute | solution.py:15
  371.5 5.2 %collective-permute-start.10 = (f32[16,4,128]{2,1,0:T(4,128)S(1)}, f32[16,4,128]{2,1,0:T(4,128)S(1)}, u32[]{:S(2)}, u32[]{:S(2)}) collective-permute-start(f32[16,4,128]{2,1,0:T(4,128)S(1)} %get-tuple-element.13), channel_id=1, source_target_pairs={{1,0},{2,1},{3,2},{4,3},{5,4},{6,5},{7,6},{8,7},{9,8},{10,9},{11,1... | collective-permute-start | bytes 98312 | tf_op jit(solution)/shard_map/ppermute | solution.py:15
  377.4 15.0 %copy-start.1 = (f32[16,32,128]{2,1,0:T(8,128)}, f32[16,32,128]{2,1,0:T(8,128)S(1)}, u32[]{:S(2)}) copy-start(f32[16,32,128]{2,1,0:T(8,128)S(1)} %fusion.48) | copy-start | bytes 786436
  377.4 9.7 %collective-permute-start.15 = (f32[16,4,128]{2,1,0:T(4,128)S(1)}, f32[16,4,128]{2,1,0:T(4,128)S(1)}, u32[]{:S(2)}, u32[]{:S(2)}) collective-permute-start(f32[16,4,128]{2,1,0:T(4,128)S(1)} %get-tuple-element.12), channel_id=1, source_target_pairs={{0,1},{1,2},{2,3},{3,4},{4,5},{5,6},{6,7},{7,8},{8,9},{9,10},{10,1... | collective-permute-start | bytes 98312 | tf_op jit(solution)/shard_map/ppermute | solution.py:15
  380.5 6.7 %collective-permute-start.14 = (f32[16,4,128]{2,1,0:T(4,128)S(1)}, f32[16,4,128]{2,1,0:T(4,128)S(1)}, u32[]{:S(2)}, u32[]{:S(2)}) collective-permute-start(f32[16,4,128]{2,1,0:T(4,128)S(1)} %get-tuple-element.11), channel_id=1, source_target_pairs={{1,0},{2,1},{3,2},{4,3},{5,4},{6,5},{7,6},{8,7},{9,8},{10,9},{11,1... | collective-permute-start | bytes 98312 | tf_op jit(solution)/shard_map/ppermute | solution.py:15
  382.4 4.8 %collective-permute-start.13 = (f32[4,32,128]{2,1,0:T(8,128)S(1)}, f32[4,32,128]{2,1,0:T(8,128)S(1)}, u32[]{:S(2)}, u32[]{:S(2)}) collective-permute-start(f32[4,32,128]{2,1,0:T(8,128)S(1)} %get-tuple-element.10), channel_id=1, source_target_pairs={{0,4},{1,5},{2,6},{3,7},{4,8},{5,9},{6,10},{7,11},{8,12},{9,13},{1... | collective-permute-start | bytes 196616 | tf_op jit(solution)/shard_map/ppermute | solution.py:15
  385.8 5.0 %collective-permute-start.12 = (f32[4,32,128]{2,1,0:T(8,128)S(1)}, f32[4,32,128]{2,1,0:T(8,128)S(1)}, u32[]{:S(2)}, u32[]{:S(2)}) collective-permute-start(f32[4,32,128]{2,1,0:T(8,128)S(1)} %get-tuple-element.9), channel_id=1, source_target_pairs={{4,0},{5,1},{6,2},{7,3},{8,4},{9,5},{10,6},{11,7},{12,8},{13,9},{1... | collective-permute-start | bytes 196616 | tf_op jit(solution)/shard_map/ppermute | solution.py:15
where the time goes:
time: 396 us; the launch traced here: 392 us
  other arithmetic  194 us (49%)
  local copies, waits for them, and re-layouts  106 us (27%)
  blocking collectives  42.7 us (11%)
  starting transfers between devices  38.7 us (10%)
  waiting for transfers between devices  9.49 us (2%)
    scatter-add x1, other arithmetic, per_device(): jnp.zeros((step_count, cell_count), jnp.float32).at[:, target].add(values)  187 us
    slice x1, local copies, waits for them, and re-layouts, per_device(): following = 2.0 * present - before + velocity * curvature + sources[moment]  72.3 us
    ppermute x16, starting transfers between devices, passed_along(): return lax.ppermute(array, axis, pairs)  38.7 us
    all_gather x1, blocking collectives, per_device(): lax.all_gather(places, 'gx', axis=1, tiled=True)  23.9 us
    scatter x1, local copies, waits for them, and re-layouts, per_device(): jnp.zeros((traces,), jnp.int32).at[where_listed]  23 us
    all_gather x1, blocking collectives, per_device(): lax.all_gather(residual_kept, 'gx', axis=1, tiled=True)  18.9 us
    ppermute x16, waiting for transfers between devices, passed_along(): return lax.ppermute(array, axis, pairs)  9.49 us
    select_n x1, local copies, waits for them, and re-layouts, per_device(): values = jnp.where(owned[None, :], gathered, 0.0)  8.44 us
  transfers between devices with their start and end apart: 16, of which 3 were waited for; matrix products, arithmetic and copies ran while one was open for 75% of the time, Pallas kernels for 0%

commit v1 on v0

v1 whole, which is shorter than its diff:
```python
import functools

import jax
import jax.numpy as jnp
from jax import lax
from jax.experimental import pallas as pl
from jax.experimental.pallas import tpu as pltpu
from jax.sharding import PartitionSpec as P

PY = 4
LANES = 128
ROWS = 8
GROUP = 4

weights = (-205.0 / 72.0, 8.0 / 5.0, -1.0 / 5.0, 8.0 / 315.0, -1.0 / 560.0)


def kernel(
    n,
    now_ref,
    before_ref,
    vel_ref,
    accel_ref,
    residual_ref,
    cell_ref,
    list_ref,
    count_ref,
    final_ref,
    prior_ref,
    gradient_ref,
    table,
    packed,
    arrived,
    field,
    sources,
    halo_send,
    halo_recv,
    trace_send,
    trace_recv,
):
    steps, cx, cy, nz = accel_ref.shape
    traces = residual_ref.shape[1]
    slots = list_ref.shape[1]
    me = lax.axis_index("gx")
    spot = me % PY

    barrier = pltpu.get_barrier_semaphore()

    def greet(j, carry):
        pl.semaphore_signal(barrier, inc=1, device_id={"gx": (me + j) % n})
        return carry

    lax.fori_loop(1, n, greet, 0)

    field[0, 4 : 4 + cx, 8 : 8 + cy] = now_ref[...]

    has = (me + PY < n, me - PY >= 0, spot < PY - 1, spot > 0)
    gets = (has[1], has[0], has[3], has[2])
    target = ((me + PY) % n, (me - PY + n) % n, (me + 1) % n, (me - 1 + n) % n)
    inside_y = pl.ds(8, cy)
    inside_x = pl.ds(4, cx)
    source_of = (
        (pl.ds(cx, 4), inside_y),
        (pl.ds(4, 4), inside_y),
        (inside_x, pl.ds(cy, 8)),
        (inside_x, pl.ds(8, 8)),
    )
    place_of = (
        (pl.ds(0, 4), inside_y),
        (pl.ds(cx + 4, 4), inside_y),
        (inside_x, pl.ds(0, 8)),
        (inside_x, pl.ds(cy + 8, 8)),
    )

    def halo_copy(s, way):
        return pltpu.make_async_remote_copy(
            src_ref=field.at[(s,) + source_of[way]],
            dst_ref=field.at[(s,) + place_of[way]],
            send_sem=halo_send.at[s, way],
            recv_sem=halo_recv.at[s, way],
            device_id={"gx": target[way]},
        )

    def send_halo(s, way):
        @pl.when(has[way])
        def _():
            halo_copy(s, way).start()

    def wait_halo(s, way):
        @pl.when(gets[way])
        def _():
            halo_copy(s, way).wait_recv()

    for way in range(4):

        @pl.when(jnp.logical_not(gets[way]))
        def _():
            for s in range(steps):
                place = field.at[(s,) + place_of[way]]
                place[...] = jnp.zeros(place.shape, jnp.float32)

    table[0:steps] = residual_ref[...]
    table[steps : steps + 1] = cell_ref[...].astype(jnp.float32)
    table[steps + 1 :] = jnp.zeros((ROWS - steps - 1, traces), jnp.float32)
    count = count_ref[0]
    row = lax.broadcasted_iota(jnp.int32, (ROWS, LANES), 0)

    def pack(t, carry):
        tile = list_ref[pl.ds(pl.multiple_of(t * ROWS, ROWS), ROWS)]
        for r in range(ROWS):
            for k in range(0, slots, LANES):
                listed = jnp.broadcast_to(tile[r : r + 1, k : k + LANES], (ROWS, LANES))
                high = listed >> 7
                low = listed & (LANES - 1)
                found = jnp.zeros((ROWS, LANES), jnp.float32)
                for h in range(traces // LANES):
                    taken = jnp.take_along_axis(
                        table[:, h * LANES : (h + 1) * LANES],
                        low,
                        axis=1,
                        mode="promise_in_bounds",
                    )
                    found = jnp.where(high == h, taken, found)
                kept = (listed < count) | (row >= steps)
                packed[t * ROWS + r, :, k : k + LANES] = jnp.where(kept, found, 0.0)
        return carry

    lax.fori_loop(0, n // ROWS, pack, 0)

    pl.semaphore_wait(barrier, n - 1)

    for way in range(4):
        send_halo(0, way)

    def trace_copy(e):
        return pltpu.make_async_remote_copy(
            src_ref=packed.at[e],
            dst_ref=arrived.at[me],
            send_sem=trace_send.at[e],
            recv_sem=trace_recv.at[me],
            device_id={"gx": e},
        )

    def send_traces(j, carry):
        trace_copy((me + j) % n).start()
        return carry

    lax.fori_loop(1, n, send_traces, 0)
    arrived[me] = packed[me]

    def wait_traces(sender):
        pltpu.make_async_remote_copy(
            src_ref=packed.at[sender],
            dst_ref=arrived.at[sender],
            send_sem=trace_send.at[sender],
            recv_sem=trace_recv.at[sender],
            device_id={"gx": sender},
        ).wait_recv()

    cells = cx * cy
    span = GROUP * slots
    high_index = lax.broadcasted_iota(jnp.int32, (cells, span), 0)
    low_index = lax.broadcasted_iota(jnp.int32, (nz, span), 0)

    def inject(half):
        def add_group(g, carry):
            senders = [(me + g * GROUP + j) % n for j in range(GROUP)]
            if half == 0:
                for sender in senders:

                    @pl.when(sender != me)
                    def _():
                        wait_traces(sender)

            block = jnp.concatenate([arrived[sender] for sender in senders], axis=1)
            cell = block[steps : steps + 1].astype(jnp.int32)
            high = (cell >> 7)
            low = cell & (LANES - 1)
            ones = jnp.where(high_index == high, 1.0, 0.0).astype(jnp.bfloat16)
            at_low = low_index == low
            coarse, fine = [], []
            for s in (2 * half, 2 * half + 1):
                value = block[s : s + 1]
                top = value.astype(jnp.bfloat16).astype(jnp.float32)
                coarse.append(jnp.where(at_low, top, 0.0).astype(jnp.bfloat16))
                fine.append(jnp.where(at_low, value - top, 0.0).astype(jnp.bfloat16))
            total = 0.0
            for part in (coarse, fine):
                total += lax.dot_general(
                    ones,
                    jnp.concatenate(part, axis=0),
                    (((1,), (1,)), ((), ())),
                    preferred_element_type=jnp.float32,
                )
            for j in range(2):
                sources[2 * half + j] += total[:, j * nz : (j + 1) * nz]
            return carry

        for j in range(2):
            sources[2 * half + j] = jnp.zeros((cells, nz), jnp.float32)
        lax.fori_loop(0, n // GROUP, add_group, 0)

    lane = lax.broadcasted_iota(jnp.int32, (1, nz), 1)
    up = [jnp.where(lane >= k, weights[k], 0.0) for k in range(1, 5)]
    down = [jnp.where(lane < nz - k, weights[k], 0.0) for k in range(1, 5)]

    def advance(s, first, last):
        def plane(x, carry):
            present = field[s, x + 4, 8 : 8 + cy]
            total = 3.0 * weights[0] * present
            for k in range(1, 5):
                pairs = field[s, x + 4 + k, 8 : 8 + cy] + field[s, x + 4 - k, 8 : 8 + cy]
                pairs += field[s, x + 4, 8 + k : 8 + k + cy]
                pairs += field[s, x + 4, 8 - k : 8 - k + cy]
                total += weights[k] * pairs
                total += up[k - 1] * pltpu.roll(present, k, 1)
                total += down[k - 1] * pltpu.roll(present, nz - k, 1)
            old = before_ref[x] if s == 0 else field[s - 1, x + 4, 8 : 8 + cy]
            here = pl.ds(pl.multiple_of(x * cy, cy), cy)
            following = 2.0 * present - old + vel_ref[x] * total + sources[s, here]
            if s + 1 < steps:
                field[s + 1, x + 4, 8 : 8 + cy] = following
            else:
                final_ref[x] = following
                prior_ref[x] = present
            term = following * accel_ref[s, x].astype(jnp.float32)
            gradient_ref[x] = term if s == 0 else gradient_ref[x] + term
            return carry

        lax.fori_loop(first, last, plane, 0)

    inject(0)
    for s in range(steps):
        for way in range(4):
            wait_halo(s, way)
        advance(s, 0, 4)
        if s + 1 < steps:
            send_halo(s + 1, 1)
        advance(s, cx - 4, cx)
        if s + 1 < steps:
            send_halo(s + 1, 0)
        advance(s, 4, cx - 4)
        if s + 1 < steps:
            send_halo(s + 1, 2)
            send_halo(s + 1, 3)
        if s == 0:
            inject(1)

    def finish(j, carry):
        trace_copy((me + j) % n).wait_send()
        return carry

    lax.fori_loop(1, n, finish, 0)
    for s in range(steps):
        for way in range(4):

            @pl.when(has[way])
            def _():
                halo_copy(s, way).wait_send()


def per_device(
    adjoint_now,
    adjoint_before,
    vel_coeff,
    forward_accel,
    residual,
    rec_cell,
    owner_list,
    trace_count,
):
    n = lax.axis_size("gx")
    steps, _, cx, cy, nz = forward_accel.shape
    traces = residual.shape[1]
    short = -owner_list.shape[1] % LANES
    lists = owner_list
    if short:
        lists = jnp.pad(owner_list, ((0, 0), (0, short)), constant_values=-1)
    slots = lists.shape[1]
    whole = pl.BlockSpec(memory_space=pltpu.VMEM)
    shape = jax.ShapeDtypeStruct((cx, cy, nz), jnp.float32)
    final, prior, gradient = pl.pallas_call(
        functools.partial(kernel, n),
        out_shape=(shape, shape, shape),
        in_specs=[whole] * 7 + [pl.BlockSpec(memory_space=pltpu.SMEM)],
        out_specs=(whole, whole, whole),
        scratch_shapes=[
            pltpu.VMEM((ROWS, traces), jnp.float32),
            pltpu.VMEM((n, ROWS, slots), jnp.float32),
            pltpu.VMEM((n, ROWS, slots), jnp.float32),
            pltpu.VMEM((steps, cx + 8, cy + 16, nz), jnp.float32),
            pltpu.VMEM((steps, cx * cy, nz), jnp.float32),
            pltpu.SemaphoreType.DMA((steps, 4)),
            pltpu.SemaphoreType.DMA((steps, 4)),
            pltpu.SemaphoreType.DMA((n,)),
            pltpu.SemaphoreType.DMA((n,)),
        ],
        compiler_params=pltpu.CompilerParams(
            collective_id=0, has_side_effects=True, vmem_limit_bytes=48 * 1024 * 1024
        ),
    )(
        adjoint_now[0],
        adjoint_before[0],
        vel_coeff[0],
        forward_accel[:, 0],
        residual,
        rec_cell[None],
        lists,
        trace_count,
    )
    return final[None], prior[None], gradient[None]


def solution(mesh):
    in_specs = (
        P(("shot", "gx"), None, None, None),
        P(("shot", "gx"), None, None, None),
        P("gx", None, None, None),
        P("shot", "gx", None, None, None),
        P("shot", "gx"),
        P("gx"),
        P("gx", None),
        P(("shot", "gx")),
    )
    out_specs = (
        P(("shot", "gx"), None, None, None),
        P(("shot", "gx"), None, None, None),
        P(("shot", "gx"), None, None, None),
    )
    return jax.shard_map(
        per_device, mesh=mesh, in_specs=in_specs, out_specs=out_specs, check_vma=False
    )
```

time: 396 us -> 43 us (0.11)
  other arithmetic: 194 us -> 0 us
  local copies, waits for them, and re-layouts: 106 us -> 7.52 us
  blocking collectives: 42.7 us -> 0 us
  starting transfers between devices: 38.7 us -> 0 us
  Pallas kernels: 0 us -> 33.7 us
  waiting for transfers between devices: 9.49 us -> 0 us
    scatter-add x1 -> x0, other arithmetic: 187 us -> none  [per_device(): jnp.zeros((step_count, cell_count), jnp.float32).at[:, target].add(values)]
    slice x9 -> x0, local copies, waits for them, and re-layouts: 74.2 us -> none  [the longest x1 72.3 us: per_device(): following = 2.0 * present - before + velocity * curvature + sources[moment]]
    all_gather x2 -> x0, blocking collectives: 42.7 us -> none  [the longest x1 23.9 us: per_device(): lax.all_gather(places, 'gx', axis=1, tiled=True)]
    ppermute x16 -> x0, starting transfers between devices: 38.7 us -> none  [passed_along(): return lax.ppermute(array, axis, pairs)]
    pallas_call x0 -> x1, Pallas kernels: none -> 33.7 us  [per_device(): pl.pallas_call(functools.partial(kernel, n), out_shape=(shape, shape, sha...]
    scatter x1 -> x0, local copies, waits for them, and re-layouts: 23 us -> none  [per_device(): jnp.zeros((traces,), jnp.int32).at[where_listed]]
    ppermute x16 -> x0, waiting for transfers between devices: 9.49 us -> none  [passed_along(): return lax.ppermute(array, axis, pairs)]
    select_n x1 -> x0, local copies, waits for them, and re-layouts: 8.44 us -> none  [per_device(): values = jnp.where(owned[None, :], gathered, 0.0)]
  transfers between devices with their start and end apart: 16 -> 0, of which waited for: 3 -> 0; matrix products, arithmetic and copies ran while one was open for 75% -> 0% of each run, Pallas kernels for 0% -> 0%
where the time goes in v1:
time: 43 us; the launch traced here: 42.5 us
  Pallas kernels  33.7 us (78%)
  local copies, waits for them, and re-layouts  7.52 us (17%)
  between operations  1.32 us (3%)
    pallas_call x1, Pallas kernels, per_device(): pl.pallas_call(functools.partial(kernel, n), out_shape=(shape, shape, sha...  33.7 us
    unnamed x17, local copies, waits for them, and re-layouts  7.52 us

profile of v1, /device:TPU:1, one launch (start us, length us, event | category | flops | bytes accessed | tf_op | source)
XLA Modules:
  0.0 42.5 jit_solution(8728251020560649552)
XLA Ops:
  0.6 0.0 copy-start.6
  1.3 0.0 copy-done.6
  1.3 0.0 copy-start
  1.3 1.0 %copy-done = bf16[4,1,16,32,128]{4,3,2,1,0:T(8,128)(2,1)S(1)} copy-done((bf16[4,1,16,32,128]{4,3,2,1,0:T(8,128)(2,1)S(1)}, bf16[4,1,16,32,128]{4,3,2,1,0:T(8,128)(2,1)}, u32[]{:S(2)}) %copy-start) | copy-done | bytes 524312
  2.4 0.0 copy-start.1
  2.4 0.9 %copy-done.1 = f32[1,16,32,128]{3,2,1,0:T(8,128)S(1)} copy-done((f32[1,16,32,128]{3,2,1,0:T(8,128)S(1)}, f32[1,16,32,128]{3,2,1,0:T(8,128)}, u32[]{:S(2)}) %copy-start.1) | copy-done | bytes 262168
  3.3 0.0 copy-start.2
  3.3 0.9 %copy-done.2 = f32[1,16,32,128]{3,2,1,0:T(8,128)S(1)} copy-done((f32[1,16,32,128]{3,2,1,0:T(8,128)S(1)}, f32[1,16,32,128]{3,2,1,0:T(8,128)}, u32[]{:S(2)}) %copy-start.2) | copy-done | bytes 262168
  4.3 0.0 copy-start.3
  4.3 0.9 %copy-done.3 = f32[1,16,32,128]{3,2,1,0:T(8,128)S(1)} copy-done((f32[1,16,32,128]{3,2,1,0:T(8,128)S(1)}, f32[1,16,32,128]{3,2,1,0:T(8,128)}, u32[]{:S(2)}) %copy-start.3) | copy-done | bytes 262168
  5.2 0.0 copy-start.4
  5.2 0.8 %copy-done.4 = f32[4,2048]{1,0:T(4,128)S(1)} copy-done((f32[4,2048]{1,0:T(4,128)S(1)}, f32[4,2048]{1,0:T(4,128)}, u32[]{:S(2)}) %copy-start.4) | copy-done | bytes 32792
  6.0 0.0 copy-start.5
  6.0 0.7 %copy-done.5 = s32[16,384]{1,0:T(8,128)S(1)} copy-done((s32[16,384]{1,0:T(8,128)S(1)}, s32[16,384]{1,0:T(8,128)}, u32[]{:S(2)}) %copy-start.5) | copy-done | bytes 24600
  6.7 33.7 %shard_map.103 = (f32[16,32,128]{2,1,0:T(8,128)S(1)}, f32[16,32,128]{2,1,0:T(8,128)S(1)}, f32[16,32,128]{2,1,0:T(8,128)S(1)}) custom-call(f32[16,32,128]{2,1,0:T(8,128)S(1)} %bitcast.9, f32[16,32,128]{2,1,0:T(8,128)S(1)} %bitcast.10, f32[16,32,128]{2,1,0:T(8,128)S(1)} %bitcast.11, bf16[4,16,32,128]{3,2,1,0:T(8,128)(2,1)S(1)} %bitcast.8, ...), custom_call_target="tpu_custom_call" | custom-call | tf_op jit(solution)/shard_map/pallas_call | solution.py:282
  40.4 0.7 %copy.15 = f32[1,16,32,128]{3,2,1,0:T(8,128)} copy(f32[1,16,32,128]{3,2,1,0:T(8,128)S(1)} %bitcast.14) | data formatting | bytes 524288
  41.1 0.7 %copy.16 = f32[1,16,32,128]{3,2,1,0:T(8,128)} copy(f32[1,16,32,128]{3,2,1,0:T(8,128)S(1)} %bitcast.13) | data formatting | bytes 524288
  41.8 0.7 %copy.17 = f32[1,16,32,128]{3,2,1,0:T(8,128)} copy(f32[1,16,32,128]{3,2,1,0:T(8,128)S(1)} %bitcast.12) | data formatting | bytes 524288
Async XLA Ops:
  0.6 0.7 %copy-start.6 = (s32[2048]{0:T(1024)S(1)}, s32[2048]{0:T(1024)}, u32[]{:S(2)}) copy-start(s32[2048]{0:T(1024)} %param.13) | copy-start | bytes 24580
  1.3 1.0 %copy-start = (bf16[4,1,16,32,128]{4,3,2,1,0:T(8,128)(2,1)S(1)}, bf16[4,1,16,32,128]{4,3,2,1,0:T(8,128)(2,1)}, u32[]{:S(2)}) copy-start(bf16[4,1,16,32,128]{4,3,2,1,0:T(8,128)(2,1)} %param.11) | copy-start | bytes 1572868
  2.4 0.9 %copy-start.1 = (f32[1,16,32,128]{3,2,1,0:T(8,128)S(1)}, f32[1,16,32,128]{3,2,1,0:T(8,128)}, u32[]{:S(2)}) copy-start(f32[1,16,32,128]{3,2,1,0:T(8,128)} %param.8) | copy-start | bytes 786436
  3.3 0.9 %copy-start.2 = (f32[1,16,32,128]{3,2,1,0:T(8,128)S(1)}, f32[1,16,32,128]{3,2,1,0:T(8,128)}, u32[]{:S(2)}) copy-start(f32[1,16,32,128]{3,2,1,0:T(8,128)} %param.9) | copy-start | bytes 786436
  4.3 0.9 %copy-start.3 = (f32[1,16,32,128]{3,2,1,0:T(8,128)S(1)}, f32[1,16,32,128]{3,2,1,0:T(8,128)}, u32[]{:S(2)}) copy-start(f32[1,16,32,128]{3,2,1,0:T(8,128)} %param.10) | copy-start | bytes 786436
  5.2 0.8 %copy-start.4 = (f32[4,2048]{1,0:T(4,128)S(1)}, f32[4,2048]{1,0:T(4,128)}, u32[]{:S(2)}) copy-start(f32[4,2048]{1,0:T(4,128)} %residual_ref.1) | copy-start | bytes 98308
  6.0 0.7 %copy-start.5 = (s32[16,384]{1,0:T(8,128)S(1)}, s32[16,384]{1,0:T(8,128)}, u32[]{:S(2)}) copy-start(s32[16,384]{1,0:T(8,128)} %list_ref.1) | copy-start | bytes 73732

commit v2 on v1

--- a/solution.py
+++ b/solution.py
@@ -11,23 +11,30 @@
 LANES = 128
 ROWS = 8
 GROUP = 4
+VMEM = 63 * 1024 * 1024
 
 weights = (-205.0 / 72.0, 8.0 / 5.0, -1.0 / 5.0, 8.0 / 315.0, -1.0 / 560.0)
 
 
 def kernel(
     n,
-    now_ref,
+    now_hbm,
+    before_hbm,
+    vel_hbm,
+    accel_hbm,
+    residual_hbm,
+    cell_hbm,
+    list_hbm,
+    count_ref,
+    final_ref,
+    prior_ref,
+    gradient_ref,
     before_ref,
     vel_ref,
     accel_ref,
     residual_ref,
     cell_ref,
     list_ref,
-    count_ref,
-    final_ref,
-    prior_ref,
-    gradient_ref,
     table,
     packed,
     arrived,
@@ -37,6 +44,7 @@
     halo_recv,
     trace_send,
     trace_recv,
+    load_sem,
 ):
     steps, cx, cy, nz = accel_ref.shape
     traces = residual_ref.shape[1]
@@ -52,7 +60,22 @@
 
     lax.fori_loop(1, n, greet, 0)
 
-    field[0, 4 : 4 + cx, 8 : 8 + cy] = now_ref[...]
+    loads = [
+        pltpu.make_async_copy(there, here, load_sem.at[i])
+        for i, (there, here) in enumerate(
+            (
+                (list_hbm, list_ref),
+                (residual_hbm, residual_ref),
+                (cell_hbm, cell_ref),
+                (now_hbm, field.at[0, 4 : 4 + cx, 8 : 8 + cy]),
+                (before_hbm, before_ref),
+                (vel_hbm, vel_ref),
+                (accel_hbm, accel_ref),
+            )
+        )
+    ]
+    for load in loads:
+        load.start()
 
     has = (me + PY < n, me - PY >= 0, spot < PY - 1, spot > 0)
     gets = (has[1], has[0], has[3], has[2])
@@ -99,6 +122,13 @@
                 place = field.at[(s,) + place_of[way]]
                 place[...] = jnp.zeros(place.shape, jnp.float32)
 
+    loads[3].wait()
+    pl.semaphore_wait(barrier, n - 1)
+    for way in range(4):
+        send_halo(0, way)
+
+    for load in loads[:3]:
+        load.wait()
     table[0:steps] = residual_ref[...]
     table[steps : steps + 1] = cell_ref[...].astype(jnp.float32)
     table[steps + 1 :] = jnp.zeros((ROWS - steps - 1, traces), jnp.float32)
@@ -127,11 +157,6 @@
 
     lax.fori_loop(0, n // ROWS, pack, 0)
 
-    pl.semaphore_wait(barrier, n - 1)
-
-    for way in range(4):
-        send_halo(0, way)
-
     def trace_copy(e):
         return pltpu.make_async_remote_copy(
             src_ref=packed.at[e],
@@ -162,7 +187,7 @@
     high_index = lax.broadcasted_iota(jnp.int32, (cells, span), 0)
     low_index = lax.broadcasted_iota(jnp.int32, (nz, span), 0)
 
-    def inject(half):
+    def inject(half, first, last):
         def add_group(g, carry):
             senders = [(me + g * GROUP + j) % n for j in range(GROUP)]
             if half == 0:
@@ -196,9 +221,7 @@
                 sources[2 * half + j] += total[:, j * nz : (j + 1) * nz]
             return carry
 
-        for j in range(2):
-            sources[2 * half + j] = jnp.zeros((cells, nz), jnp.float32)
-        lax.fori_loop(0, n // GROUP, add_group, 0)
+        lax.fori_loop(first, last, add_group, 0)
 
     lane = lax.broadcasted_iota(jnp.int32, (1, nz), 1)
     up = [jnp.where(lane >= k, weights[k], 0.0) for k in range(1, 5)]
@@ -215,36 +238,61 @@
                 total += weights[k] * pairs
                 total += up[k - 1] * pltpu.roll(present, k, 1)
                 total += down[k - 1] * pltpu.roll(present, nz - k, 1)
+            here = pl.ds(pl.multiple_of(x * cy, cy), cy)
             old = before_ref[x] if s == 0 else field[s - 1, x + 4, 8 : 8 + cy]
-            here = pl.ds(pl.multiple_of(x * cy, cy), cy)
-            following = 2.0 * present - old + vel_ref[x] * total + sources[s, here]
+            following = 2.0 * present - old + vel_ref[x] * total
+            if s == 0:
+                sources[0, here] = following
+                return carry
+            following += sources[s, here]
             if s + 1 < steps:
                 field[s + 1, x + 4, 8 : 8 + cy] = following
             else:
                 final_ref[x] = following
                 prior_ref[x] = present
-            term = following * accel_ref[s, x].astype(jnp.float32)
-            gradient_ref[x] = term if s == 0 else gradient_ref[x] + term
+            gradient_ref[x] += following * accel_ref[s, x].astype(jnp.float32)
             return carry
 
         lax.fori_loop(first, last, plane, 0)
 
-    inject(0)
+    def begin(s, first, last):
+        def plane(x, carry):
+            here = pl.ds(pl.multiple_of(x * cy, cy), cy)
+            following = sources[0, here]
+            field[1, x + 4, 8 : 8 + cy] = following
+            gradient_ref[x] = following * accel_ref[0, x].astype(jnp.float32)
+            return carry
+
+        lax.fori_loop(first, last, plane, 0)
+
+    for s in range(1, steps):
+        sources[s] = jnp.zeros((cells, nz), jnp.float32)
+    for load in loads[4:]:
+        load.wait()
+    for way in range(4):
+        wait_halo(0, way)
+    advance(0, 0, cx)
+    groups = n // GROUP
+    inject(0, 0, groups)
     for s in range(steps):
-        for way in range(4):
-            wait_halo(s, way)
-        advance(s, 0, 4)
+        if s:
+            for way in range(4):
+                wait_halo(s, way)
+        move = advance if s else begin
+        move(s, 0, 4)
         if s + 1 < steps:
             send_halo(s + 1, 1)
-        advance(s, cx - 4, cx)
+        move(s, cx - 4, cx)
         if s + 1 < steps:
             send_halo(s + 1, 0)
-        advance(s, 4, cx - 4)
+        move(s, 4, cx - 4)
         if s + 1 < steps:
             send_halo(s + 1, 2)
             send_halo(s + 1, 3)
         if s == 0:
-            inject(1)
+            inject(1, 0, groups // 2)
+        if s == 1:
+            inject(1, groups // 2, groups)
 
     def finish(j, carry):
         trace_copy((me + j) % n).wait_send()
@@ -257,6 +305,15 @@
             @pl.when(has[way])
             def _():
                 halo_copy(s, way).wait_send()
+
+
+def write_out(final_ref, prior_ref, gradient_ref, final_hbm, prior_hbm, gradient_hbm, sem):
+    pairs = ((final_ref, final_hbm), (prior_ref, prior_hbm), (gradient_ref, gradient_hbm))
+    copies = [pltpu.make_async_copy(a, b, sem.at[i]) for i, (a, b) in enumerate(pairs)]
+    for copy in copies:
+        copy.start()
+    for copy in copies:
+        copy.wait()
 
 
 def per_device(
@@ -277,14 +334,21 @@
     if short:
         lists = jnp.pad(owner_list, ((0, 0), (0, short)), constant_values=-1)
     slots = lists.shape[1]
+    far = pl.BlockSpec(memory_space=pltpu.HBM)
     whole = pl.BlockSpec(memory_space=pltpu.VMEM)
     shape = jax.ShapeDtypeStruct((cx, cy, nz), jnp.float32)
     final, prior, gradient = pl.pallas_call(
         functools.partial(kernel, n),
         out_shape=(shape, shape, shape),
-        in_specs=[whole] * 7 + [pl.BlockSpec(memory_space=pltpu.SMEM)],
+        in_specs=[far] * 7 + [pl.BlockSpec(memory_space=pltpu.SMEM)],
         out_specs=(whole, whole, whole),
         scratch_shapes=[
+            pltpu.VMEM((cx, cy, nz), jnp.float32),
+            pltpu.VMEM((cx, cy, nz), jnp.float32),
+            pltpu.VMEM((steps, cx, cy, nz), forward_accel.dtype),
+            pltpu.VMEM(residual.shape, jnp.float32),
+            pltpu.VMEM((1, traces), jnp.int32),
+            pltpu.VMEM(lists.shape, jnp.int32),
             pltpu.VMEM((ROWS, traces), jnp.float32),
             pltpu.VMEM((n, ROWS, slots), jnp.float32),
             pltpu.VMEM((n, ROWS, slots), jnp.float32),
@@ -294,9 +358,10 @@
             pltpu.SemaphoreType.DMA((steps, 4)),
             pltpu.SemaphoreType.DMA((n,)),
             pltpu.SemaphoreType.DMA((n,)),
+            pltpu.SemaphoreType.DMA((7,)),
         ],
         compiler_params=pltpu.CompilerParams(
-            collective_id=0, has_side_effects=True, vmem_limit_bytes=48 * 1024 * 1024
+            collective_id=0, has_side_effects=True, vmem_limit_bytes=VMEM
         ),
     )(
         adjoint_now[0],
@@ -308,6 +373,14 @@
         lists,
         trace_count,
     )
+    final, prior, gradient = pl.pallas_call(
+        write_out,
+        out_shape=(shape, shape, shape),
+        in_specs=[far] * 3,
+        out_specs=(far, far, far),
+        scratch_shapes=[pltpu.SemaphoreType.DMA((3,))],
+        compiler_params=pltpu.CompilerParams(vmem_limit_bytes=VMEM),
+    )(final, prior, gradient)
     return final[None], prior[None], gradient[None]
 
 

time: 43 us -> 58.8 us (1.37)
  Pallas kernels: 33.7 us -> 57.3 us
  local copies, waits for them, and re-layouts: 7.52 us -> 0 us
    pallas_call x0 -> x1, Pallas kernels: none -> 25 us  [per_device(): pl.pallas_call(write_out, out_shape=(shape, shape, shape), in_specs=[far]...]
    unnamed x17 -> x0, local copies, waits for them, and re-layouts: 7.52 us -> none
    pallas_call x1, Pallas kernels: 33.7 us -> 32.4 us  [per_device(): pl.pallas_call(functools.partial(kernel, n), out_shape=(shape, shape, sha...]
where the time goes in v2:
time: 58.8 us; the launch traced here: 58.6 us
  Pallas kernels  57.3 us (97%)
  between operations  1.29 us (2%)
    pallas_call x1, Pallas kernels, per_device(): pl.pallas_call(functools.partial(kernel, n), out_shape=(shape, shape, sha...  32.4 us
    pallas_call x1, Pallas kernels, per_device(): pl.pallas_call(write_out, out_shape=(shape, shape, shape), in_specs=[far]...  25 us

profile of v2, /device:TPU:1, one launch (start us, length us, event | category | flops | bytes accessed | tf_op | source)
XLA Modules:
  0.0 58.6 jit_solution(2068698148060450943)
XLA Ops:
  1.3 32.4 %shard_map.103 = (f32[16,32,128]{2,1,0:T(8,128)}, f32[16,32,128]{2,1,0:T(8,128)}, f32[16,32,128]{2,1,0:T(8,128)}) custom-call(f32[16,32,128]{2,1,0:T(8,128)} %bitcast.9, f32[16,32,128]{2,1,0:T(8,128)} %bitcast.10, f32[16,32,128]{2,1,0:T(8,128)} %bitcast.11, bf16[4,16,32,128]{3,2,1,0:T(8,128)(2,1)} %bitcast.8, f32[4,2048]{1,0:T(4,128)} %residual_hbm.1, ...), custom_call_target="tpu_custom_call" | custom-call | tf_op jit(solution)/shard_map/pallas_call | solution.py:340
  33.7 25.0 %shard_map.104 = (f32[16,32,128]{2,1,0:T(8,128)}, f32[16,32,128]{2,1,0:T(8,128)}, f32[16,32,128]{2,1,0:T(8,128)}) custom-call(f32[16,32,128]{2,1,0:T(8,128)} %get-tuple-element.9.final_ref, f32[16,32,128]{2,1,0:T(8,128)} %get-tuple-element.10.prior_ref, f32[16,32,128]{2,1,0:T(8,128)} %get-tuple-element.11.gradient_ref), custom_call_target="tpu_custom_call" | custom-call | tf_op jit(solution)/shard_map/pallas_call | solution.py:376

commit v3 on v2

--- a/solution.py
+++ b/solution.py
@@ -85,14 +85,14 @@
     source_of = (
         (pl.ds(cx, 4), inside_y),
         (pl.ds(4, 4), inside_y),
-        (inside_x, pl.ds(cy, 8)),
-        (inside_x, pl.ds(8, 8)),
+        (inside_x, pl.ds(cy + 4, 4)),
+        (inside_x, pl.ds(8, 4)),
     )
     place_of = (
         (pl.ds(0, 4), inside_y),
         (pl.ds(cx + 4, 4), inside_y),
-        (inside_x, pl.ds(0, 8)),
-        (inside_x, pl.ds(cy + 8, 8)),
+        (inside_x, pl.ds(4, 4)),
+        (inside_x, pl.ds(cy + 8, 4)),
     )
 
     def halo_copy(s, way):
@@ -132,6 +132,9 @@
     table[0:steps] = residual_ref[...]
     table[steps : steps + 1] = cell_ref[...].astype(jnp.float32)
     table[steps + 1 :] = jnp.zeros((ROWS - steps - 1, traces), jnp.float32)
+    used = slots // LANES * (steps + 1)
+    if packed.shape[1] > used:
+        packed[:, used:] = jnp.zeros((n, packed.shape[1] - used, LANES), jnp.float32)
     count = count_ref[0]
     row = lax.broadcasted_iota(jnp.int32, (ROWS, LANES), 0)
 
@@ -152,7 +155,10 @@
                     )
                     found = jnp.where(high == h, taken, found)
                 kept = (listed < count) | (row >= steps)
-                packed[t * ROWS + r, :, k : k + LANES] = jnp.where(kept, found, 0.0)
+                first = k // LANES * (steps + 1)
+                packed[t * ROWS + r, first : first + steps + 1] = jnp.where(kept, found, 0.0)[
+                    : steps + 1
+                ]
         return carry
 
     lax.fori_loop(0, n // ROWS, pack, 0)
@@ -197,15 +203,20 @@
                     def _():
                         wait_traces(sender)
 
-            block = jnp.concatenate([arrived[sender] for sender in senders], axis=1)
-            cell = block[steps : steps + 1].astype(jnp.int32)
+            blocks = [arrived[sender] for sender in senders]
+
+            def line(r):
+                starts = range(r, slots // LANES * (steps + 1), steps + 1)
+                return jnp.concatenate([b[i : i + 1] for b in blocks for i in starts], axis=1)
+
+            cell = line(steps).astype(jnp.int32)
             high = (cell >> 7)
             low = cell & (LANES - 1)
             ones = jnp.where(high_index == high, 1.0, 0.0).astype(jnp.bfloat16)
             at_low = low_index == low
             coarse, fine = [], []
             for s in (2 * half, 2 * half + 1):
-                value = block[s : s + 1]
+                value = line(s)
                 top = value.astype(jnp.bfloat16).astype(jnp.float32)
                 coarse.append(jnp.where(at_low, top, 0.0).astype(jnp.bfloat16))
                 fine.append(jnp.where(at_low, value - top, 0.0).astype(jnp.bfloat16))
@@ -307,13 +318,18 @@
                 halo_copy(s, way).wait_send()
 
 
-def write_out(final_ref, prior_ref, gradient_ref, final_hbm, prior_hbm, gradient_hbm, sem):
-    pairs = ((final_ref, final_hbm), (prior_ref, prior_hbm), (gradient_ref, gradient_hbm))
-    copies = [pltpu.make_async_copy(a, b, sem.at[i]) for i, (a, b) in enumerate(pairs)]
-    for copy in copies:
-        copy.start()
-    for copy in copies:
-        copy.wait()
+def write_out(final_in, prior_in, gradient_in, final_out, prior_out, gradient_out, held, sem):
+    ins = (final_in, prior_in, gradient_in)
+    outs = (final_out, prior_out, gradient_out)
+    loads = [pltpu.make_async_copy(ins[i], held.at[i], sem.at[0, i]) for i in range(3)]
+    stores = [pltpu.make_async_copy(held.at[i], outs[i], sem.at[1, i]) for i in range(3)]
+    for load in loads:
+        load.start()
+    for i in range(3):
+        loads[i].wait()
+        stores[i].start()
+    for store in stores:
+        store.wait()
 
 
 def per_device(
@@ -334,6 +350,7 @@
     if short:
         lists = jnp.pad(owner_list, ((0, 0), (0, short)), constant_values=-1)
     slots = lists.shape[1]
+    lines = -(-(slots // LANES * (steps + 1)) // ROWS) * ROWS
     far = pl.BlockSpec(memory_space=pltpu.HBM)
     whole = pl.BlockSpec(memory_space=pltpu.VMEM)
     shape = jax.ShapeDtypeStruct((cx, cy, nz), jnp.float32)
@@ -350,8 +367,8 @@
             pltpu.VMEM((1, traces), jnp.int32),
             pltpu.VMEM(lists.shape, jnp.int32),
             pltpu.VMEM((ROWS, traces), jnp.float32),
-            pltpu.VMEM((n, ROWS, slots), jnp.float32),
-            pltpu.VMEM((n, ROWS, slots), jnp.float32),
+            pltpu.VMEM((n, lines, LANES), jnp.float32),
+            pltpu.VMEM((n, lines, LANES), jnp.float32),
             pltpu.VMEM((steps, cx + 8, cy + 16, nz), jnp.float32),
             pltpu.VMEM((steps, cx * cy, nz), jnp.float32),
             pltpu.SemaphoreType.DMA((steps, 4)),
@@ -378,7 +395,7 @@
         out_shape=(shape, shape, shape),
         in_specs=[far] * 3,
         out_specs=(far, far, far),
-        scratch_shapes=[pltpu.SemaphoreType.DMA((3,))],
+        scratch_shapes=[pltpu.VMEM((3, cx, cy, nz), jnp.float32), pltpu.SemaphoreType.DMA((2, 3))],
         compiler_params=pltpu.CompilerParams(vmem_limit_bytes=VMEM),
     )(final, prior, gradient)
     return final[None], prior[None], gradient[None]

time: 58.8 us -> 34 us (0.58)
  Pallas kernels: 57.3 us -> 32.6 us
    pallas_call x1, Pallas kernels: 25 us -> 1.88 us  [per_device(): pl.pallas_call(write_out, out_shape=(shape, shape, shape), in_specs=[far]...]
    pallas_call x1, Pallas kernels: 32.4 us -> 30.7 us  [per_device(): pl.pallas_call(functools.partial(kernel, n), out_shape=(shape, shape, sha...]
where the time goes in v3:
time: 34 us; the launch traced here: 33.9 us
  Pallas kernels  32.6 us (96%)
  between operations  1.29 us (4%)
    pallas_call x1, Pallas kernels, per_device(): pl.pallas_call(functools.partial(kernel, n), out_shape=(shape, shape, sha...  30.7 us
    pallas_call x1, Pallas kernels, per_device(): pl.pallas_call(write_out, out_shape=(shape, shape, shape), in_specs=[far]...  1.88 us

profile of v3, /device:TPU:1, one launch (start us, length us, event | category | flops | bytes accessed | tf_op | source)
XLA Modules:
  0.0 33.9 jit_solution(15446872235221867856)
XLA Ops:
  1.3 30.7 %shard_map.103 = (f32[16,32,128]{2,1,0:T(8,128)}, f32[16,32,128]{2,1,0:T(8,128)}, f32[16,32,128]{2,1,0:T(8,128)}) custom-call(f32[16,32,128]{2,1,0:T(8,128)} %bitcast.9, f32[16,32,128]{2,1,0:T(8,128)} %bitcast.10, f32[16,32,128]{2,1,0:T(8,128)} %bitcast.11, bf16[4,16,32,128]{3,2,1,0:T(8,128)(2,1)} %bitcast.8, f32[4,2048]{1,0:T(4,128)} %residual_hbm.1, ...), custom_call_target="tpu_custom_call" | custom-call | tf_op jit(solution)/shard_map/pallas_call | solution.py:357
  32.0 1.9 %shard_map.104 = (f32[16,32,128]{2,1,0:T(8,128)}, f32[16,32,128]{2,1,0:T(8,128)}, f32[16,32,128]{2,1,0:T(8,128)}) custom-call(f32[16,32,128]{2,1,0:T(8,128)} %get-tuple-element.9.final_in, f32[16,32,128]{2,1,0:T(8,128)} %get-tuple-element.10.prior_in, f32[16,32,128]{2,1,0:T(8,128)} %get-tuple-element.11.gradient_in), custom_call_target="tpu_custom_call" | custom-call | tf_op jit(solution)/shard_map/pallas_call | solution.py:393

commit v4 on v3

--- a/solution.py
+++ b/solution.py
@@ -173,7 +173,7 @@
         )
 
     def send_traces(j, carry):
-        trace_copy((me + j) % n).start()
+        trace_copy((me + n - j) % n).start()
         return carry
 
     lax.fori_loop(1, n, send_traces, 0)
@@ -264,7 +264,7 @@
             gradient_ref[x] += following * accel_ref[s, x].astype(jnp.float32)
             return carry
 
-        lax.fori_loop(first, last, plane, 0)
+        lax.fori_loop(first, last, plane, 0, unroll=4)
 
     def begin(s, first, last):
         def plane(x, carry):
@@ -274,7 +274,7 @@
             gradient_ref[x] = following * accel_ref[0, x].astype(jnp.float32)
             return carry
 
-        lax.fori_loop(first, last, plane, 0)
+        lax.fori_loop(first, last, plane, 0, unroll=4)
 
     for s in range(1, steps):
         sources[s] = jnp.zeros((cells, nz), jnp.float32)

time: 34 us -> 31.5 us (0.926); the launches traced: 33.9 us -> 31 us
  Pallas kernels: 32.6 us -> 29.7 us
    pallas_call x1, Pallas kernels: 30.7 us -> 27.8 us  [per_device(): pl.pallas_call(functools.partial(kernel, n), out_shape=(shape, shape, sha...]
where the time goes in v4:
time: 31.5 us; the launch traced here: 31 us
  Pallas kernels  29.7 us (94%)
  between operations  1.29 us (4%)
    pallas_call x1, Pallas kernels, per_device(): pl.pallas_call(functools.partial(kernel, n), out_shape=(shape, shape, sha...  27.8 us
    pallas_call x1, Pallas kernels, per_device(): pl.pallas_call(write_out, out_shape=(shape, shape, shape), in_specs=[far]...  1.88 us

profile of v4, /device:TPU:1, one launch (start us, length us, event | category | flops | bytes accessed | tf_op | source)
XLA Modules:
  0.0 31.0 jit_solution(2822600302558720085)
XLA Ops:
  1.3 27.8 %shard_map.103 = (f32[16,32,128]{2,1,0:T(8,128)}, f32[16,32,128]{2,1,0:T(8,128)}, f32[16,32,128]{2,1,0:T(8,128)}) custom-call(f32[16,32,128]{2,1,0:T(8,128)} %bitcast.9, f32[16,32,128]{2,1,0:T(8,128)} %bitcast.10, f32[16,32,128]{2,1,0:T(8,128)} %bitcast.11, bf16[4,16,32,128]{3,2,1,0:T(8,128)(2,1)} %bitcast.8, f32[4,2048]{1,0:T(4,128)} %residual_hbm.1, ...), custom_call_target="tpu_custom_call" | custom-call | tf_op jit(solution)/shard_map/pallas_call | solution.py:357
  29.1 1.9 %shard_map.104 = (f32[16,32,128]{2,1,0:T(8,128)}, f32[16,32,128]{2,1,0:T(8,128)}, f32[16,32,128]{2,1,0:T(8,128)}) custom-call(f32[16,32,128]{2,1,0:T(8,128)} %get-tuple-element.9.final_in, f32[16,32,128]{2,1,0:T(8,128)} %get-tuple-element.10.prior_in, f32[16,32,128]{2,1,0:T(8,128)} %get-tuple-element.11.gradient_in), custom_call_target="tpu_custom_call" | custom-call | tf_op jit(solution)/shard_map/pallas_call | solution.py:393

commit v5 on v4

--- a/solution.py
+++ b/solution.py
@@ -264,7 +264,7 @@
             gradient_ref[x] += following * accel_ref[s, x].astype(jnp.float32)
             return carry
 
-        lax.fori_loop(first, last, plane, 0, unroll=4)
+        lax.fori_loop(first, last, plane, 0, unroll=True)
 
     def begin(s, first, last):
         def plane(x, carry):
@@ -274,7 +274,7 @@
             gradient_ref[x] = following * accel_ref[0, x].astype(jnp.float32)
             return carry
 
-        lax.fori_loop(first, last, plane, 0, unroll=4)
+        lax.fori_loop(first, last, plane, 0, unroll=True)
 
     for s in range(1, steps):
         sources[s] = jnp.zeros((cells, nz), jnp.float32)
@@ -287,12 +287,14 @@
     inject(0, 0, groups)
     for s in range(steps):
         if s:
-            for way in range(4):
+            for way in (0, 2, 3):
                 wait_halo(s, way)
         move = advance if s else begin
         move(s, 0, 4)
         if s + 1 < steps:
             send_halo(s + 1, 1)
+        if s:
+            wait_halo(s, 1)
         move(s, cx - 4, cx)
         if s + 1 < steps:
             send_halo(s + 1, 0)

time: 31.5 us -> 31.1 us (0.987)
  no operation moved by 1% of the time
where the time goes in v5:
time: 31.1 us; the launch traced here: 30.8 us
  Pallas kernels  29.5 us (95%)
  between operations  1.29 us (4%)
    pallas_call x1, Pallas kernels, per_device(): pl.pallas_call(functools.partial(kernel, n), out_shape=(shape, shape, sha...  27.6 us
    pallas_call x1, Pallas kernels, per_device(): pl.pallas_call(write_out, out_shape=(shape, shape, shape), in_specs=[far]...  1.88 us

profile of v5, /device:TPU:1, one launch (start us, length us, event | category | flops | bytes accessed | tf_op | source)
XLA Modules:
  0.0 30.8 jit_solution(999299979789095098)
XLA Ops:
  1.3 27.6 %shard_map.103 = (f32[16,32,128]{2,1,0:T(8,128)}, f32[16,32,128]{2,1,0:T(8,128)}, f32[16,32,128]{2,1,0:T(8,128)}) custom-call(f32[16,32,128]{2,1,0:T(8,128)} %bitcast.9, f32[16,32,128]{2,1,0:T(8,128)} %bitcast.10, f32[16,32,128]{2,1,0:T(8,128)} %bitcast.11, bf16[4,16,32,128]{3,2,1,0:T(8,128)(2,1)} %bitcast.8, f32[4,2048]{1,0:T(4,128)} %residual_hbm.1, ...), custom_call_target="tpu_custom_call" | custom-call | tf_op jit(solution)/shard_map/pallas_call | solution.py:359
  28.9 1.9 %shard_map.104 = (f32[16,32,128]{2,1,0:T(8,128)}, f32[16,32,128]{2,1,0:T(8,128)}, f32[16,32,128]{2,1,0:T(8,128)}) custom-call(f32[16,32,128]{2,1,0:T(8,128)} %get-tuple-element.9.final_in, f32[16,32,128]{2,1,0:T(8,128)} %get-tuple-element.10.prior_in, f32[16,32,128]{2,1,0:T(8,128)} %get-tuple-element.11.gradient_in), custom_call_target="tpu_custom_call" | custom-call | tf_op jit(solution)/shard_map/pallas_call | solution.py:395
